TPU v7x, 32 devices: a whole 2x2x4 slice. The times are simulated.
32 devices in a mesh: groups: 2 (over y), col: 4 (over z), row: 4 (over x, core).
Axes of the slice: x: 2, y: 2, z: 4, core: 2. Of those that a mesh axis runs over, the one named last changes fastest.
Arguments:
- pair_slab: bfloat16 [128, 512, 128], P(('groups', 'row'), 'col'), parts along dimension 0, may hold values from -6 to 6
- tile_pair: bfloat16 [8, 2, 128, 128, 128], P(('groups', 'col'), None, 'row'), parts along dimension 0, may hold values from -6 to 6
- tile_cotan: bfloat16 [8, 2, 128, 128, 128], P(('groups', 'col'), None, 'row'), parts along dimension 0, may hold values from -6 to 6
- tile_rows: int32 [8, 2], P(('groups', 'col')), parts along dimension 0, may hold values from 0 to 3, as said below
- tile_count: int32 [8], P(('groups', 'col')), parts along dimension 0, may hold values from 1 to 2, as said below
- norm_gain: float32 [128], replicated, may hold values from 0.5 to 1.5
- norm_bias: float32 [128], replicated, may hold values from -2.5 to 2.5
- w_in: bfloat16 [128, 512], replicated, may hold values from -0.5 to 0.5
- out_gain: float32 [128], replicated, may hold values from 0.5 to 1.5
- out_bias: float32 [128], replicated, may hold values from -2.5 to 2.5
- w_out: bfloat16 [128, 128], replicated, may hold values from -0.5 to 0.5
- w_gate: bfloat16 [128, 128], replicated, may hold values from -0.5 to 0.5
Outputs:
- update: bfloat16 [8, 2, 128, 128, 128], P(('groups', 'col'), None, 'row'), parts along dimension 0
- grad_slab: bfloat16 [128, 512, 128], P(('groups', 'row'), 'col'), parts along dimension 0
- grad_tiles: bfloat16 [8, 2, 128, 128, 128], P(('groups', 'col'), None, 'row'), parts along dimension 0
- grad_in_w: float32 [256, 512], P('groups'), parts along dimension 0
- grad_out_w: float32 [256, 128], P('groups'), parts along dimension 0
- grad_gate_w: float32 [256, 128], P('groups'), parts along dimension 0
There are 2 independent parts, one for each index of `groups`. A program takes and returns all parts, laid end to end along the dimension named above; an argument that names none is the same for every part. Nothing has to cross between parts.
Inputs may be any that keep to these rules, and one draw needn't show every extreme that they name: `tile_count`: every column block has at least one active slot and some column block has all 2 active. `tile_rows`: the row blocks named by the slots of one column block are distinct; slots at or past the count are inactive.
All inputs are finite; a program needn't handle non-finite values.
Results may differ from a plain program's by a relative error of at most 0.015.
Values may be sent and summed in bfloat16 or wider, within the bound.
A program may use at most 128 MiB of HBM per device.

v0:
```python
import jax
import jax.numpy as jnp
from jax import lax
from jax.sharding import PartitionSpec as P

epsilon = 1e-05


def normalize(values):
    center = values - jnp.mean(values, axis=-1, keepdims=True)
    variance = jnp.mean(center * center, axis=-1, keepdims=True)
    inverse = lax.rsqrt(variance + epsilon)
    return (center * inverse, inverse)


def norm_back(grad_in, centred, inverse, gain):
    scaled = grad_in * gain
    first = jnp.mean(scaled, axis=-1, keepdims=True)
    second = jnp.mean(scaled * centred, axis=-1, keepdims=True)
    return inverse * (scaled - first - centred * second)


def rounded(values):
    return lax.optimization_barrier(values.astype(jnp.bfloat16)).astype(jnp.float32)


def body(
    pair_slab,
    tile_pair,
    tile_cotan,
    tile_rows,
    tile_count,
    norm_gain,
    norm_bias,
    w_in,
    out_gain,
    out_bias,
    w_out,
    w_gate,
):
    k_local, tile_len, channels = pair_slab.shape
    hidden_w = w_out.shape[0]
    slots = tile_rows.shape[1]
    row_count = lax.axis_size("row")
    col_count = lax.axis_size("col")
    row_part = tile_len // row_count
    slab_hat, slab_inv = normalize(pair_slab.astype(jnp.float32))
    slab_norm = (slab_hat * norm_gain + norm_bias).astype(jnp.bfloat16)
    flat_norm = slab_norm.reshape(-1, channels)
    project = jnp.dot(flat_norm, w_in, preferred_element_type=jnp.float32).reshape(
        k_local, tile_len, 4 * hidden_w
    )
    left_proj = project[..., :hidden_w]
    left_sig = jax.nn.sigmoid(project[..., hidden_w : 2 * hidden_w])
    right_proj = project[..., 2 * hidden_w : 3 * hidden_w]
    right_sig = jax.nn.sigmoid(project[..., 3 * hidden_w :])
    left_edges = (left_sig * left_proj).astype(jnp.bfloat16)
    right_edges = (right_sig * right_proj).astype(jnp.bfloat16)
    row_blocks = tile_rows[0]
    active = (jnp.arange(slots) < tile_count[0]).astype(jnp.float32)
    selector = (row_blocks[:, None] == jnp.arange(col_count)[None, :]).astype(jnp.float32) * active[
        :, None
    ]
    spread = lax.all_to_all(
        left_edges.reshape(k_local, row_count, row_part, hidden_w),
        "row",
        split_axis=1,
        concat_axis=0,
        tiled=True,
    )
    panels = lax.all_gather(spread, "col", axis=1, tiled=True)
    chosen = jnp.take(panels, row_blocks, axis=1)
    right_full = lax.all_gather(right_edges, "row", axis=0, tiled=True)
    grouped = jnp.einsum(
        "gksih,gkjh->gsijh",
        chosen.reshape(row_count, k_local, slots, row_part, hidden_w),
        right_full.reshape(row_count, k_local, tile_len, hidden_w),
        preferred_element_type=jnp.float32,
    )
    combined = jnp.sum(rounded(grouped), axis=0)
    comb_hat, comb_inv = normalize(combined)
    comb_norm = (comb_hat * out_gain + out_bias).astype(jnp.bfloat16)
    pair_hat, pair_inv = normalize(tile_pair[0].astype(jnp.float32))
    pair_norm = (pair_hat * norm_gain + norm_bias).astype(jnp.bfloat16)
    flat_comb = comb_norm.reshape(-1, hidden_w)
    flat_pair = pair_norm.reshape(-1, channels)
    mixed = jnp.dot(flat_comb, w_out, preferred_element_type=jnp.float32)
    gate = jax.nn.sigmoid(jnp.dot(flat_pair, w_gate, preferred_element_type=jnp.float32))
    row_mask = jnp.repeat(active, row_part * tile_len)[:, None]
    update = (row_mask * gate * mixed).astype(jnp.bfloat16)
    cotan = tile_cotan[0].astype(jnp.float32).reshape(-1, channels) * row_mask
    grad_mixed = (cotan * gate).astype(jnp.bfloat16)
    grad_logit = (cotan * mixed * gate * (1.0 - gate)).astype(jnp.bfloat16)
    grad_out_w = jnp.dot(flat_comb.T, grad_mixed, preferred_element_type=jnp.float32)
    grad_gate_w = jnp.dot(flat_pair.T, grad_logit, preferred_element_type=jnp.float32)
    out_total, gate_total = (grad_out_w, grad_gate_w)
    grad_comb = jnp.dot(grad_mixed, w_out.T, preferred_element_type=jnp.float32).reshape(
        slots, row_part, tile_len, hidden_w
    )
    grad_pair = jnp.dot(grad_logit, w_gate.T, preferred_element_type=jnp.float32).reshape(
        slots, row_part, tile_len, channels
    )
    pair_back = norm_back(grad_pair, pair_hat, pair_inv, norm_gain).astype(jnp.bfloat16)
    comb_back = norm_back(grad_comb, comb_hat, comb_inv, out_gain).astype(jnp.bfloat16)
    left_term = rounded(
        jnp.einsum("sijh,kjh->ksih", comb_back, right_full, preferred_element_type=jnp.float32)
    )
    routed = jnp.einsum("ksih,sb->kbih", left_term, selector)
    column_sum = lax.psum_scatter(
        routed.astype(jnp.bfloat16), "col", scatter_dimension=1, tiled=True
    ).astype(jnp.float32)
    returned = lax.all_to_all(
        column_sum.reshape(row_count, k_local, row_part, hidden_w).astype(jnp.bfloat16),
        "row",
        split_axis=0,
        concat_axis=2,
        tiled=True,
    ).astype(jnp.float32)
    left_grad = returned.reshape(k_local, tile_len, hidden_w)
    right_part = jnp.einsum(
        "sijh,ksih->skjh", comb_back, chosen, preferred_element_type=jnp.float32
    )
    right_grad = jnp.sum(
        lax.psum_scatter(
            right_part.astype(jnp.bfloat16), "row", scatter_dimension=1, tiled=True
        ).astype(jnp.float32),
        axis=0,
    )
    grad_project = jnp.concatenate(
        [
            left_grad * left_sig,
            left_grad * left_proj * left_sig * (1.0 - left_sig),
            right_grad * right_sig,
            right_grad * right_proj * right_sig * (1.0 - right_sig),
        ],
        axis=-1,
    ).astype(jnp.bfloat16)
    flat_grad = grad_project.reshape(-1, 4 * hidden_w)
    grad_in_w = jnp.dot(flat_norm.T, flat_grad, preferred_element_type=jnp.float32)
    grad_norm = jnp.dot(flat_grad, w_in.T, preferred_element_type=jnp.float32).reshape(
        k_local, tile_len, channels
    )
    grad_slab = norm_back(grad_norm, slab_hat, slab_inv, norm_gain).astype(jnp.bfloat16)
    in_total, out_total, gate_total = lax.psum((grad_in_w, out_total, gate_total), ("col", "row"))
    update_out = update.reshape(1, slots, row_part, tile_len, channels)
    tiles_out = pair_back.reshape(1, slots, row_part, tile_len, channels)
    return (update_out, grad_slab, tiles_out, in_total, out_total, gate_total)


def solution(mesh):
    return jax.shard_map(
        body,
        mesh=mesh,
        in_specs=(
            P(("groups", "row"), "col", None),
            P(("groups", "col"), None, "row", None, None),
            P(("groups", "col"), None, "row", None, None),
            P(("groups", "col"), None),
            P(("groups", "col")),
            P(),
            P(),
            P(),
            P(),
            P(),
            P(),
            P(),
        ),
        out_specs=(
            P(("groups", "col"), None, "row", None, None),
            P(("groups", "row"), "col", None),
            P(("groups", "col"), None, "row", None, None),
            P("groups", None),
            P("groups", None),
            P("groups", None),
        ),
        check_vma=False,
    )
```

profile of v0, /device:TPU:0, one launch (start us, length us, event | category | flops | bytes accessed | tf_op | source)
XLA Modules:
  0.0 365.0 jit_solution(873537648331085904)
XLA Ops:
  7.2 1.3 copy.55
  8.7 0.2 fusion.25
  8.9 1.5 fusion.33
  10.4 1.9 copy-done.1
  12.3 1.3 multiply_convert_fusion.7
  13.7 0.8 copy.57
  14.5 4.2 %all-to-all-start = ((bf16[16,4,32,128]{3,2,0,1:T(8,128)(2,1)}), bf16[16,4,32,128]{3,2,0,1:T(8,128)(2,1)S(1)}, u32[]{:S(2)}, u32[]{:S(2)}) async-start(bf16[16,4,32,128]{3,2,0,1:T(8,128)(2,1)} %copy.57), calls=%async_computation | async-start | bytes 1048576 | tf_op jit(solution)/shard_map/all_to_all | solution.py:64
  19.5 9.8 %all-to-all-done = bf16[16,4,32,128]{3,2,0,1:T(8,128)(2,1)S(1)} async-done(((bf16[16,4,32,128]{3,2,0,1:T(8,128)(2,1)}), bf16[16,4,32,128]{3,2,0,1:T(8,128)(2,1)S(1)}, u32[]{:S(2)}, u32[]{:S(2)}) %all-to-all-start) | async-done | bytes 524320 | tf_op jit(solution)/shard_map/all_to_all | solution.py:64
  29.3 0.8 copy-done.11
  30.2 0.6 convert_reduce_fusion.2
  30.9 2.5 fusion.11
  33.4 3.5 add_convert_fusion.1
  36.9 3.4 all-gather.3.cloned.1.call-done
  40.3 4.5 %copy.74 = bf16[4,16,128,128,1]{2,1,4,3,0:T(8,128)(2,1)} copy(bf16[4,16,128,128,1]{3,2,1,0,4:T(8,128)(2,1)} %bitcast.112) | data formatting | bytes 4194304 | tf_op jit(solution)/shard_map/reshape | solution.py:77
  44.8 4.2 %copy.75 = bf16[64,128,128,1]{1,0,3,2:T(8,128)(2,1)} copy(bf16[64,128,128,1]{2,1,0,3:T(8,128)(2,1)} %bitcast.113) | data formatting | bytes 4194304 | tf_op jit(solution)/shard_map/all_gather | solution.py:73
  49.0 40.4 %all-gather.5.cloned.1.call-done = bf16[64,4,32,128]{3,2,1,0:T(8,128)(2,1)} async-done(((bf16[64,1,32,128]{3,2,1,0:T(8,128)(2,1)}), bf16[64,4,32,128]{3,2,1,0:T(8,128)(2,1)}) %all-gather.5.cloned.1.call-update) | async-done | bytes 2097168 | tf_op jit(solution)/shard_map/all_gather | solution.py:71
  89.5 3.3 gather_fusion
  92.7 1.4 copy.59
  94.1 1.1 broadcast_select_fusion.1
  95.2 7.2 %copy.61 = bf16[4,16,2,32,128]{3,1,2,4,0:T(8,128)(2,1)} copy(bf16[4,16,2,32,128]{4,3,2,1,0:T(8,128)(2,1)} %broadcast_select_fusion.1) | data formatting | bytes 2097152 | tf_op jit(solution)/shard_map/jit(_take)/select_n | solution.py:72
  102.4 5.2 %convert_bitcast_fusion = bf16[4,2,32,128,128]{3,2,1,4,0:T(8,128)(2,1)S(1)} fusion(bf16[4,16,128,128,1]{2,1,4,3,0:T(8,128)(2,1)} %copy.74, bf16[4,16,2,32,128]{3,1,2,4,0:T(8,128)(2,1)} %copy.61), kind=kOutput, calls=%fused_computation.7 | convolution fusion | flops 138412032 | bytes 11534336 | tf_op jit(solution)/shard_map/gksih,gkjh->gsijh/dot_general | solution.py:74
  107.7 5.1 %convert_reduce_fusion = (f32[2,32,128]{2,1,0:T(8,128)S(1)}, f32[2,32,128,128]{2,1,0,3:T(8,128)}) fusion(bf16[4,2,32,128,128]{3,2,1,4,0:T(8,128)(2,1)S(1)} %convert_bitcast_fusion), kind=kLoop, calls=%fused_computation.1 | loop fusion | flops 11526144 | bytes 12615680 | tf_op jit(solution)/shard_map/reduce_sum | solution.py:10
  112.7 5.3 %copy.62 = f32[2,32,128,128]{3,2,1,0:T(8,128)} copy(f32[2,32,128,128]{2,1,0,3:T(8,128)} %get-tuple-element.31) | data formatting | bytes 8388608 | tf_op jit(solution)/shard_map/reduce_sum | solution.py:80
  118.1 2.8 multiply_reduce_fusion.2
  120.9 0.6 copy-done.2
  121.5 4.5 %add_convert_fusion = bf16[8192,128]{1,0:T(8,128)(2,1)S(1)} fusion(f32[2,32,128,128]{3,2,1,0:T(8,128)S(1)} %copy-done.2, f32[128]{0:T(128)S(1)} %copy-done.18, f32[128]{0:T(128)S(1)} %copy-done.15, f32[8192]{0:T(1024)S(1)} %bitcast.123, f32[8192]{0:T(1024)S(1)} %bitcast.119), kind=kLoop, calls=%fused_computation.28 | loop fusion | flops 5242880 | bytes 6358016 | tf_op jit(solution)/shard_map/convert_element_type | solution.py:82
  126.1 0.7 fusion.48
  126.8 0.6 copy-done.4
  127.4 1.0 copy-done.7
  128.4 0.6 copy-done.19
  129.1 4.3 %fusion.8 = (bf16[8192,128]{1,0:T(8,128)(2,1)}, bf16[8192,128]{1,0:T(8,128)(2,1)}, bf16[8192,128]{1,0:T(8,128)(2,1)S(1)}) fusion(f32[8192,128]{1,0:T(8,128)S(1)} %fusion.48, bf16[1,2,32,128,128]{4,3,2,1,0:T(8,128)(2,1)S(1)} %copy-done.19, f32[8192]{0:T(1024)S(1)} %bitcast.132, bf16[8192,128]{1,0:T(8,128)(2,1)S(1)} %copy-done.7, ...), kind=kOutput, calls=%fused_computation.14 | convolution fusion | flops 284164096 | bytes 14745600 | tf_op jit(solution)/shard_map/dot_general | solution.py:88
  133.4 6.2 %multiply_reduce_fusion.4 = (f32[8192]{0:T(1024)S(1)}, f32[8192]{0:T(1024)S(1)}, f32[8192,128]{1,0:T(8,128)}) fusion(f32[128]{0:T(128)S(1)} %copy-done.15, f32[8192]{0:T(1024)S(1)} %bitcast.124, f32[8192]{0:T(1024)S(1)} %bitcast.120, f32[2,32,128,128]{3,2,1,0:T(8,128)S(1)} %copy-done.2, bf16[8192,128]{1,0:T(8,128)(2,1)S(1)} %get-tuple-element.43, ...), kind=kOutput, calls=%fused_computation.32 | convolution fusion | flops 274710528 | bytes 10650112 | tf_op jit(solution)/shard_map/dot_general | solution.py:97
  139.6 5.5 %copy.63 = f32[2,32,128,128]{2,1,0,3:T(8,128)} copy(f32[2,32,128,128]{3,2,1,0:T(8,128)} %bitcast.110) | data formatting | bytes 8388608 | tf_op jit(solution)/shard_map/reshape | solution.py:97
  145.1 4.8 %multiply_convert_fusion.1 = bf16[2,32,128,128]{2,1,0,3:T(8,128)(2,1)S(1)} fusion(f32[2,32,128,128]{2,1,0,3:T(8,128)} %copy.63, f32[2,32,128,128]{2,1,0,3:T(8,128)} %get-tuple-element.31, f32[2,32,128]{2,1,0:T(8,128)S(1)} %bitcast.128, f32[2,32,128]{2,1,0:T(8,128)S(1)} %bitcast.129, f32[128]{0:T(128)S(1)} %copy-done.15, f32[2,32,128]{2,1,0:T(8,128)S(1)} %add_rsqrt_fusion, ...), kind=kLoop, calls=%fused_computation.25 | loop fusion | flops 8388608 | bytes 10617344 | tf_op jit(solution)/shard_map/convert_element_type | solution.py:104
  149.9 1.4 copy-done.5
  151.3 2.5 convert_bitcast_fusion.3
  153.8 4.7 %copy.65 = bf16[64,2,32,128]{3,1,2,0:T(2,128)(2,1)} copy(bf16[64,2,32,128]{0,2,1,3:T(8,128)(2,1)} %convert_bitcast_fusion.3) | data formatting | bytes 2097152 | tf_op jit(solution)/shard_map/optimization_barrier | solution.py:24
  158.5 2.8 convert_bitcast_fusion.2
  161.3 1.7 copy.66
  163.1 2.4 broadcast_select_fusion
  165.4 5.4 %copy.68 = bf16[64,2,32,128]{0,2,3,1:T(8,128)(2,1)} copy(bf16[64,2,32,128]{3,2,0,1:T(8,128)(2,1)} %broadcast_select_fusion) | data formatting | bytes 2097152 | tf_op jit(solution)/shard_map/jit(_take)/select_n | solution.py:72
  170.8 5.5 %convert_bitcast_fusion.1 = bf16[2,64,128,128]{2,1,3,0:T(8,128)(2,1)} fusion(bf16[64,2,32,128]{0,2,3,1:T(8,128)(2,1)} %copy.68, bf16[2,32,128,128]{2,1,0,3:T(8,128)(2,1)} %copy-done.5), kind=kOutput, calls=%fused_computation.24 | convolution fusion | flops 136314880 | bytes 7340032 | tf_op jit(solution)/shard_map/sijh,ksih->skjh/dot_general | solution.py:120
  176.3 7.2 %multiply_reduce_fusion.3 = (f32[8192]{0:T(1024)S(1)}, f32[8192]{0:T(1024)S(1)}, f32[8192,128]{1,0:T(8,128)S(1)}) fusion(f32[128]{0:T(128)S(1)} %copy-done.16, f32[8192]{0:T(1024)S(1)} %bitcast.127, f32[8192]{0:T(1024)S(1)} %bitcast.122, bf16[1,2,32,128,128]{4,3,2,1,0:T(8,128)(2,1)S(1)} %copy-done.3, bf16[8192,128]{1,0:T(8,128)(2,1)} %get-tuple-element.41, ...), kind=kOutput, calls=%fused_computation.31 | convolution fusion | flops 275759104 | bytes 8552960 | tf_op jit(solution)/shard_map/dot_general | solution.py:100
  183.5 5.9 %multiply_convert_fusion = bf16[1,2,32,128,128]{4,3,2,1,0:T(8,128)(2,1)} fusion(f32[1,2,32,128,128]{4,3,2,1,0:T(8,128)S(1)} %bitcast.115, bf16[1,2,32,128,128]{4,3,2,1,0:T(8,128)(2,1)S(1)} %copy-done.3, f32[2,32,128]{2,1,0:T(8,128)S(1)} %bitcast.130, f32[2,32,128]{2,1,0:T(8,128)S(1)} %broadcast_multiply_fusion.5, f32[2,32,128]{2,1,0:T(8,128)S(1)} %bitcast.131, ...), kind=kLoop, calls=%fused_computation.22 | loop fusion | flops 9437184 | bytes 8520192 | tf_op jit(solution)/shard_map/convert_element_type | solution.py:103
  189.5 16.3 %reduce-scatter.3.cloned.1.call-done = bf16[64,1,32,128]{3,2,0,1:T(8,128)(2,1)} async-done(((bf16[64,4,32,128]{3,2,0,1:T(8,128)(2,1)}), bf16[64,1,32,128]{3,2,0,1:T(8,128)(2,1)}) %reduce-scatter.3.cloned.1.call-update) | async-done | bytes 524304 | tf_op jit(solution)/shard_map/reduce_scatter | solution.py:109
  205.8 3.5 all-to-all-start.1
  209.2 0.3 all-reduce.3.cloned.1.call-start
  209.6 3.8 %fusion.49 = f32[128,128]{1,0:T(8,128)} fusion(bf16[8192,128]{1,0:T(8,128)(2,1)} %copy-done.4, bf16[8192,128]{1,0:T(8,128)(2,1)} %copy-done.9), kind=kOutput, calls=%fused_computation.105 | convolution fusion | flops 268435456 | bytes 4259840 | tf_op jit(solution)/shard_map/dot_general | solution.py:94
  213.3 1.4 fusion.50
  214.7 3.4 all-to-all-done.1
  218.0 0.1 convert_bitcast_fusion.4
  218.3 33.9 %reduce-scatter.5.cloned.1.call-done = bf16[2,16,128,128]{2,1,3,0:T(8,128)(2,1)} async-done(((bf16[2,64,128,128]{2,1,3,0:T(8,128)(2,1)}), bf16[2,16,128,128]{2,1,3,0:T(8,128)(2,1)}) %reduce-scatter.5.cloned.1.call-update) | async-done | bytes 1048592 | tf_op jit(solution)/shard_map/reduce_scatter | solution.py:124
  252.2 1.5 convert_reduce_fusion.3
  253.7 1.4 copy.70
  255.0 3.6 multiply_convert_fusion.6
  258.7 0.8 copy-done.13
  259.4 1.2 convolution_bitcast_fusion
  260.6 2.0 fusion.47
  262.7 0.3 fusion.24
  263.0 1.0 copy.72
  264.0 89.8 %all-reduce.3.cloned.1.call-done = (f32[128,512]{1,0:T(8,128)}, f32[128,128]{1,0:T(8,128)}, f32[128,128]{1,0:T(8,128)}) async-done(((f32[128,512]{1,0:T(8,128)}, f32[128,128]{1,0:T(8,128)}, f32[128,128]{1,0:T(8,128)}), (f32[128,512]{1,0:T(8,128)}, f32[128,128]{1,0:T(8,128)}, f32[128,128]{1,0:T(8,128)})) %all-reduce.3.cloned.1.call-update) | async-done | bytes 393232 | tf_op jit(solution)/shard_map/psum | solution.py:144
  353.8 1.7 copy.88
  355.5 1.5 copy.89
  357.0 1.5 copy.90
  (63 shorter events, 0.6 us)
Async XLA Ops:
  7.2 1.7 copy-start
  7.2 33.2 %all-gather.3.cloned.1.call-start = ((), (), s32[]{:S(2)}) async-start(), calls=%async_computation.4 | async-start | bytes 2621440 | tf_op jit(solution)/shard_map/all_gather | solution.py:73
  10.4 1.9 copy-start.1
  12.3 7.2 %copy-start.21 = (s32[1,2]{1,0:T(1,128)S(1)}, s32[1,2]{1,0:T(1,128)}, u32[]{:S(2)}) copy-start(s32[1,2]{1,0:T(1,128)} %param.15) | copy-start | bytes 28
  12.3 17.9 %copy-start.3 = (bf16[1,2,32,128,128]{4,3,2,1,0:T(8,128)(2,1)S(1)}, bf16[1,2,32,128,128]{4,3,2,1,0:T(8,128)(2,1)}, u32[]{:S(2)}) copy-start(bf16[1,2,32,128,128]{4,3,2,1,0:T(8,128)(2,1)} %param.13) | copy-start | bytes 6291460
  13.7 19.8 %copy-start.16 = (f32[128]{0:T(128)S(1)}, f32[128]{0:T(128)}, u32[]{:S(2)}) copy-start(f32[128]{0:T(128)} %param.17) | copy-start | bytes 1540
  13.7 19.8 %copy-start.17 = (f32[128]{0:T(128)S(1)}, f32[128]{0:T(128)}, u32[]{:S(2)}) copy-start(f32[128]{0:T(128)} %param.18) | copy-start | bytes 1540
  14.5 14.8 %all-to-all-start = ((bf16[16,4,32,128]{3,2,0,1:T(8,128)(2,1)}), bf16[16,4,32,128]{3,2,0,1:T(8,128)(2,1)S(1)}, u32[]{:S(2)}, u32[]{:S(2)}) async-start(bf16[16,4,32,128]{3,2,0,1:T(8,128)(2,1)} %copy.57), calls=%async_computation | async-start | bytes 1048576 | tf_op jit(solution)/shard_map/all_to_all | solution.py:64
  18.7 70.7 %all-gather.5.cloned.1.call-start = ((), (), s32[]{:S(2)}) async-start(), calls=%async_computation.5 | async-start | bytes 2621440 | tf_op jit(solution)/shard_map/all_gather | solution.py:71
  29.3 0.8 copy-start.11
  30.1 175.6 %reduce-scatter.3.cloned.1.call-start = ((), (), s32[]{:S(2)}) async-start(), calls=%async_computation.6 | async-start | bytes 2621440 | tf_op jit(solution)/shard_map/reduce_scatter | solution.py:109
  118.1 3.4 copy-start.2
  118.1 3.4 copy-start.15
  118.1 3.5 copy-start.18
  120.9 5.2 %copy-start.14 = (bf16[128,128]{1,0:T(8,128)(2,1)S(1)}, bf16[128,128]{1,0:T(8,128)(2,1)}, u32[]{:S(2)}) copy-start(bf16[128,128]{1,0:T(8,128)(2,1)} %param.22) | copy-start | bytes 98308
  126.1 1.3 copy-start.4
  126.1 2.3 copy-start.7
  126.1 3.0 copy-start.19
  126.1 3.0 copy-start.20
  133.4 6.2 %copy-start.9 = (bf16[8192,128]{1,0:T(8,128)(2,1)}, bf16[8192,128]{1,0:T(8,128)(2,1)S(1)}, u32[]{:S(2)}) copy-start(bf16[8192,128]{1,0:T(8,128)(2,1)S(1)} %get-tuple-element.43) | copy-start | bytes 6291460
  145.1 6.2 %copy-start.6 = (bf16[64,128,128,1]{1,0,3,2:T(8,128)(2,1)S(1)}, bf16[64,128,128,1]{1,0,3,2:T(8,128)(2,1)}, u32[]{:S(2)}) copy-start(bf16[64,128,128,1]{1,0,3,2:T(8,128)(2,1)} %copy.75) | copy-start | bytes 6291460
  149.9 1.4 copy-start.5
  163.0 89.1 %reduce-scatter.5.cloned.1.call-start = ((), (), s32[]{:S(2)}) async-start(), calls=%async_computation.7 | async-start | bytes 5242880 | tf_op jit(solution)/shard_map/reduce_scatter | solution.py:124
  189.5 23.9 %copy-start.8 = (bf16[8192,128]{1,0:T(8,128)(2,1)S(1)}, bf16[8192,128]{1,0:T(8,128)(2,1)}, u32[]{:S(2)}) copy-start(bf16[8192,128]{1,0:T(8,128)(2,1)} %add_convert_fusion.1) | copy-start | bytes 6291460
  205.8 12.3 %all-to-all-start.1 = ((bf16[4,16,32,128]{3,2,1,0:T(8,128)(2,1)}), bf16[4,16,32,128]{3,2,1,0:T(8,128)(2,1)S(1)}, u32[]{:S(2)}, u32[]{:S(2)}) async-start(bf16[4,16,32,128]{3,2,1,0:T(8,128)(2,1)} %bitcast.125), calls=%async_computation.2 | async-start | bytes 1048576 | tf_op jit(solution)/shard_map/all_to_all | solution.py:112
  209.2 144.6 %all-reduce.3.cloned.1.call-start = ((), (), s32[]{:S(2)}) async-start(), calls=%async_computation.8 | async-start | bytes 786432 | tf_op jit(solution)/shard_map/psum | solution.py:144
  209.5 3.8 %copy-start.10 = (bf16[8192,128]{1,0:T(8,128)(2,1)S(1)}, bf16[8192,128]{1,0:T(8,128)(2,1)}, u32[]{:S(2)}) copy-start(bf16[8192,128]{1,0:T(8,128)(2,1)} %get-tuple-element.41) | copy-start | bytes 6291460
  258.6 0.8 copy-start.13
  258.7 2.0 copy-start.12
Sparse Core Ops, SparseCore 0:
  13.8 26.4 all-gather.2
  42.5 46.9 all-gather.4
  163.1 42.5 reduce-scatter.2
  208.3 43.8 reduce-scatter.4
  262.8 90.9 all-reduce.2
where the time goes:
time: 366 us; the launch traced here: 365 us
  waiting for transfers between devices  197 us (54%)
  local copies, waits for them, and re-layouts  60.2 us (16%)
  matrix products  44.3 us (12%)
  other arithmetic  40.4 us (11%)
  between operations  14.8 us (4%)
  starting transfers between devices  8.1 us (2%)
    psum x1, waiting for transfers between devices, body(): lax.psum((grad_in_w, out_total, gate_total), ('col', 'row'))  89.8 us
    all_gather x1, waiting for transfers between devices, body(): panels = lax.all_gather(spread, 'col', axis=1, tiled=True)  40.4 us
    reduce_scatter x1, waiting for transfers between devices, body(): lax.psum_scatter(right_part.astype(jnp.bfloat16), 'row', scatter_dimensio...  33.9 us
    reduce_scatter x1, waiting for transfers between devices, body(): lax.psum_scatter(routed.astype(jnp.bfloat16), 'col', scatter_dimension=1,...  16.3 us
    unnamed x51, local copies, waits for them, and re-layouts  14.8 us
    select_n x2, local copies, waits for them, and re-layouts, body(): chosen = jnp.take(panels, row_blocks, axis=1)  12.6 us
    all_to_all x1, waiting for transfers between devices, body(): lax.all_to_all(left_edges.reshape(k_local, row_count, row_part, hidden_w)...  9.82 us
  transfers between devices with their start and end apart: 7, of which 7 were waited for; matrix products, arithmetic and copies ran while one was open for 14% of the time, Pallas kernels for 0%

commit v1 on v0

--- a/solution.py
+++ b/solution.py
@@ -61,13 +61,10 @@
     selector = (row_blocks[:, None] == jnp.arange(col_count)[None, :]).astype(jnp.float32) * active[
         :, None
     ]
-    spread = lax.all_to_all(
-        left_edges.reshape(k_local, row_count, row_part, hidden_w),
-        "row",
-        split_axis=1,
-        concat_axis=0,
-        tiled=True,
-    )
+    block = left_edges.reshape(k_local, row_count, row_part, hidden_w)
+    pieces = jnp.split(block, lax.axis_size("row"), axis=1)
+    received = lax.all_to_all(jnp.stack(pieces), "row", 0, 0)
+    spread = jnp.concatenate(received, axis=0)
     panels = lax.all_gather(spread, "col", axis=1, tiled=True)
     chosen = jnp.take(panels, row_blocks, axis=1)
     right_full = lax.all_gather(right_edges, "row", axis=0, tiled=True)

time: 366 us -> 366 us (level)
  no operation moved by 1% of the time
where the time goes in v1:
time: 366 us; the launch traced here: 365 us
  waiting for transfers between devices  197 us (54%)
  local copies, waits for them, and re-layouts  59.4 us (16%)
  matrix products  44.3 us (12%)
  other arithmetic  41.3 us (11%)
  between operations  14.8 us (4%)
  starting transfers between devices  8.1 us (2%)
    psum x1, waiting for transfers between devices, body(): lax.psum((grad_in_w, out_total, gate_total), ('col', 'row'))  89.8 us
    all_gather x1, waiting for transfers between devices, body(): panels = lax.all_gather(spread, 'col', axis=1, tiled=True)  40.4 us
    reduce_scatter x1, waiting for transfers between devices, body(): lax.psum_scatter(right_part.astype(jnp.bfloat16), 'row', scatter_dimensio...  33.9 us
    reduce_scatter x1, waiting for transfers between devices, body(): lax.psum_scatter(routed.astype(jnp.bfloat16), 'col', scatter_dimension=1,...  16.3 us
    unnamed x51, local copies, waits for them, and re-layouts  14.8 us
    select_n x2, local copies, waits for them, and re-layouts, body(): chosen = jnp.take(panels, row_blocks, axis=1)  12.6 us
    all_to_all x1, waiting for transfers between devices, body(): received = lax.all_to_all(jnp.stack(pieces), 'row', 0, 0)  9.92 us
  transfers between devices with their start and end apart: 7, of which 7 were waited for; matrix products, arithmetic and copies ran while one was open for 14% of the time, Pallas kernels for 0%

profile of v1, /device:TPU:0, one launch (start us, length us, event | category | flops | bytes accessed | tf_op | source)
XLA Modules:
  0.0 365.0 jit_solution(13779066549046208919)
XLA Ops:
  7.2 1.3 copy.60
  8.7 0.2 fusion.25
  8.9 1.5 fusion.33
  10.4 1.9 copy-done.1
  12.3 1.3 multiply_convert_fusion.7
  13.7 0.9 pad_maximum_fusion.1
  14.6 4.2 %all-to-all-start = ((bf16[4,16,1,32,128]{4,3,1,2,0:T(8,128)(2,1)}), bf16[4,16,1,32,128]{4,3,1,2,0:T(8,128)(2,1)S(1)}, u32[]{:S(2)}, u32[]{:S(2)}) async-start(bf16[4,16,1,32,128]{4,3,1,2,0:T(8,128)(2,1)} %pad_maximum_fusion.1), calls=%async_computation | async-start | bytes 1048576 | tf_op jit(solution)/shard_map/all_to_all | solution.py:66
  19.6 9.9 %all-to-all-done = bf16[4,16,1,32,128]{4,3,1,2,0:T(8,128)(2,1)S(1)} async-done(((bf16[4,16,1,32,128]{4,3,1,2,0:T(8,128)(2,1)}), bf16[4,16,1,32,128]{4,3,1,2,0:T(8,128)(2,1)S(1)}, u32[]{:S(2)}, u32[]{:S(2)}) %all-to-all-start) | async-done | bytes 524320 | tf_op jit(solution)/shard_map/all_to_all | solution.py:66
  29.5 0.8 copy-done.11
  30.4 0.6 convert_reduce_fusion.2
  31.0 2.5 fusion.11
  33.6 3.5 add_convert_fusion.1
  37.1 3.3 all-gather.3.cloned.1.call-done
  40.4 4.5 %copy.80 = bf16[4,16,128,128,1]{2,1,4,3,0:T(8,128)(2,1)} copy(bf16[4,16,128,128,1]{3,2,1,0,4:T(8,128)(2,1)} %bitcast.120) | data formatting | bytes 4194304 | tf_op jit(solution)/shard_map/reshape | solution.py:74
  44.9 4.2 %copy.81 = bf16[64,128,128,1]{1,0,3,2:T(8,128)(2,1)} copy(bf16[64,128,128,1]{2,1,0,3:T(8,128)(2,1)} %bitcast.121) | data formatting | bytes 4194304 | tf_op jit(solution)/shard_map/all_gather | solution.py:70
  49.1 40.4 %all-gather.5.cloned.1.call-done = bf16[64,4,32,128]{3,2,1,0:T(8,128)(2,1)} async-done(((bf16[64,1,32,128]{3,2,1,0:T(8,128)(2,1)}), bf16[64,4,32,128]{3,2,1,0:T(8,128)(2,1)}) %all-gather.5.cloned.1.call-update) | async-done | bytes 2097168 | tf_op jit(solution)/shard_map/all_gather | solution.py:68
  89.5 3.3 gather_fusion
  92.8 1.4 copy.65
  94.2 1.1 broadcast_select_fusion.1
  95.3 7.2 %copy.67 = bf16[4,16,2,32,128]{3,1,2,4,0:T(8,128)(2,1)} copy(bf16[4,16,2,32,128]{4,3,2,1,0:T(8,128)(2,1)} %broadcast_select_fusion.1) | data formatting | bytes 2097152 | tf_op jit(solution)/shard_map/jit(_take)/select_n | solution.py:69
  102.5 5.2 %convert_bitcast_fusion = bf16[4,2,32,128,128]{3,2,1,4,0:T(8,128)(2,1)S(1)} fusion(bf16[4,16,128,128,1]{2,1,4,3,0:T(8,128)(2,1)} %copy.80, bf16[4,16,2,32,128]{3,1,2,4,0:T(8,128)(2,1)} %copy.67), kind=kOutput, calls=%fused_computation.7 | convolution fusion | flops 138412032 | bytes 11534336 | tf_op jit(solution)/shard_map/gksih,gkjh->gsijh/dot_general | solution.py:71
  107.7 5.1 %convert_reduce_fusion = (f32[2,32,128]{2,1,0:T(8,128)S(1)}, f32[2,32,128,128]{2,1,0,3:T(8,128)}) fusion(bf16[4,2,32,128,128]{3,2,1,4,0:T(8,128)(2,1)S(1)} %convert_bitcast_fusion), kind=kLoop, calls=%fused_computation.1 | loop fusion | flops 11526144 | bytes 12615680 | tf_op jit(solution)/shard_map/reduce_sum | solution.py:10
  112.8 5.3 %copy.68 = f32[2,32,128,128]{3,2,1,0:T(8,128)} copy(f32[2,32,128,128]{2,1,0,3:T(8,128)} %get-tuple-element.31) | data formatting | bytes 8388608 | tf_op jit(solution)/shard_map/reduce_sum | solution.py:77
  118.2 2.8 multiply_reduce_fusion.2
  121.0 0.6 copy-done.2
  121.6 4.5 %add_convert_fusion = bf16[8192,128]{1,0:T(8,128)(2,1)S(1)} fusion(f32[2,32,128,128]{3,2,1,0:T(8,128)S(1)} %copy-done.2, f32[128]{0:T(128)S(1)} %copy-done.18, f32[128]{0:T(128)S(1)} %copy-done.15, f32[8192]{0:T(1024)S(1)} %bitcast.131, f32[8192]{0:T(1024)S(1)} %bitcast.127), kind=kLoop, calls=%fused_computation.28 | loop fusion | flops 5242880 | bytes 6358016 | tf_op jit(solution)/shard_map/convert_element_type | solution.py:79
  126.2 0.7 fusion.48
  126.9 0.6 copy-done.4
  127.5 1.0 copy-done.7
  128.5 0.6 copy-done.19
  129.2 4.3 %fusion.8 = (bf16[8192,128]{1,0:T(8,128)(2,1)}, bf16[8192,128]{1,0:T(8,128)(2,1)}, bf16[8192,128]{1,0:T(8,128)(2,1)S(1)}) fusion(f32[8192,128]{1,0:T(8,128)S(1)} %fusion.48, bf16[1,2,32,128,128]{4,3,2,1,0:T(8,128)(2,1)S(1)} %copy-done.19, f32[8192]{0:T(1024)S(1)} %bitcast.140, bf16[8192,128]{1,0:T(8,128)(2,1)S(1)} %copy-done.7, ...), kind=kOutput, calls=%fused_computation.14 | convolution fusion | flops 284164096 | bytes 14745600 | tf_op jit(solution)/shard_map/dot_general | solution.py:85
  133.5 6.2 %multiply_reduce_fusion.4 = (f32[8192]{0:T(1024)S(1)}, f32[8192]{0:T(1024)S(1)}, f32[8192,128]{1,0:T(8,128)}) fusion(f32[128]{0:T(128)S(1)} %copy-done.15, f32[8192]{0:T(1024)S(1)} %bitcast.132, f32[8192]{0:T(1024)S(1)} %bitcast.128, f32[2,32,128,128]{3,2,1,0:T(8,128)S(1)} %copy-done.2, bf16[8192,128]{1,0:T(8,128)(2,1)S(1)} %get-tuple-element.43, ...), kind=kOutput, calls=%fused_computation.32 | convolution fusion | flops 274710528 | bytes 10650112 | tf_op jit(solution)/shard_map/dot_general | solution.py:94
  139.7 5.5 %copy.69 = f32[2,32,128,128]{2,1,0,3:T(8,128)} copy(f32[2,32,128,128]{3,2,1,0:T(8,128)} %bitcast.118) | data formatting | bytes 8388608 | tf_op jit(solution)/shard_map/reshape | solution.py:94
  145.2 4.8 %multiply_convert_fusion.1 = bf16[2,32,128,128]{2,1,0,3:T(8,128)(2,1)S(1)} fusion(f32[2,32,128,128]{2,1,0,3:T(8,128)} %copy.69, f32[2,32,128,128]{2,1,0,3:T(8,128)} %get-tuple-element.31, f32[2,32,128]{2,1,0:T(8,128)S(1)} %bitcast.136, f32[2,32,128]{2,1,0:T(8,128)S(1)} %bitcast.137, f32[128]{0:T(128)S(1)} %copy-done.15, f32[2,32,128]{2,1,0:T(8,128)S(1)} %add_rsqrt_fusion, ...), kind=kLoop, calls=%fused_computation.25 | loop fusion | flops 8388608 | bytes 10617344 | tf_op jit(solution)/shard_map/convert_element_type | solution.py:101
  150.0 1.4 copy-done.5
  151.3 2.5 convert_bitcast_fusion.3
  153.9 4.7 %copy.71 = bf16[64,2,32,128]{3,1,2,0:T(2,128)(2,1)} copy(bf16[64,2,32,128]{0,2,1,3:T(8,128)(2,1)} %convert_bitcast_fusion.3) | data formatting | bytes 2097152 | tf_op jit(solution)/shard_map/optimization_barrier | solution.py:24
  158.6 2.8 convert_bitcast_fusion.2
  161.4 1.7 copy.72
  163.1 2.4 broadcast_select_fusion
  165.5 5.4 %copy.74 = bf16[64,2,32,128]{0,2,3,1:T(8,128)(2,1)} copy(bf16[64,2,32,128]{3,2,0,1:T(8,128)(2,1)} %broadcast_select_fusion) | data formatting | bytes 2097152 | tf_op jit(solution)/shard_map/jit(_take)/select_n | solution.py:69
  170.9 5.5 %convert_bitcast_fusion.1 = bf16[2,64,128,128]{2,1,3,0:T(8,128)(2,1)} fusion(bf16[64,2,32,128]{0,2,3,1:T(8,128)(2,1)} %copy.74, bf16[2,32,128,128]{2,1,0,3:T(8,128)(2,1)} %copy-done.5), kind=kOutput, calls=%fused_computation.24 | convolution fusion | flops 136314880 | bytes 7340032 | tf_op jit(solution)/shard_map/sijh,ksih->skjh/dot_general | solution.py:117
  176.4 7.2 %multiply_reduce_fusion.3 = (f32[8192]{0:T(1024)S(1)}, f32[8192]{0:T(1024)S(1)}, f32[8192,128]{1,0:T(8,128)S(1)}) fusion(f32[128]{0:T(128)S(1)} %copy-done.16, f32[8192]{0:T(1024)S(1)} %bitcast.135, f32[8192]{0:T(1024)S(1)} %bitcast.130, bf16[1,2,32,128,128]{4,3,2,1,0:T(8,128)(2,1)S(1)} %copy-done.3, bf16[8192,128]{1,0:T(8,128)(2,1)} %get-tuple-element.41, ...), kind=kOutput, calls=%fused_computation.31 | convolution fusion | flops 275759104 | bytes 8552960 | tf_op jit(solution)/shard_map/dot_general | solution.py:97
  183.6 5.9 %multiply_convert_fusion = bf16[1,2,32,128,128]{4,3,2,1,0:T(8,128)(2,1)} fusion(f32[1,2,32,128,128]{4,3,2,1,0:T(8,128)S(1)} %bitcast.123, bf16[1,2,32,128,128]{4,3,2,1,0:T(8,128)(2,1)S(1)} %copy-done.3, f32[2,32,128]{2,1,0:T(8,128)S(1)} %bitcast.138, f32[2,32,128]{2,1,0:T(8,128)S(1)} %broadcast_multiply_fusion.5, f32[2,32,128]{2,1,0:T(8,128)S(1)} %bitcast.139, ...), kind=kLoop, calls=%fused_computation.22 | loop fusion | flops 9437184 | bytes 8520192 | tf_op jit(solution)/shard_map/convert_element_type | solution.py:100
  189.5 16.3 %reduce-scatter.3.cloned.1.call-done = bf16[64,1,32,128]{3,2,0,1:T(8,128)(2,1)} async-done(((bf16[64,4,32,128]{3,2,0,1:T(8,128)(2,1)}), bf16[64,1,32,128]{3,2,0,1:T(8,128)(2,1)}) %reduce-scatter.3.cloned.1.call-update) | async-done | bytes 524304 | tf_op jit(solution)/shard_map/reduce_scatter | solution.py:106
  205.8 3.5 all-to-all-start.1
  209.3 0.3 all-reduce.3.cloned.1.call-start
  209.6 3.8 %fusion.49 = f32[128,128]{1,0:T(8,128)} fusion(bf16[8192,128]{1,0:T(8,128)(2,1)} %copy-done.4, bf16[8192,128]{1,0:T(8,128)(2,1)} %copy-done.9), kind=kOutput, calls=%fused_computation.110 | convolution fusion | flops 268435456 | bytes 4259840 | tf_op jit(solution)/shard_map/dot_general | solution.py:91
  213.4 1.4 fusion.50
  214.7 3.3 all-to-all-done.1
  218.1 0.1 convert_bitcast_fusion.4
  218.3 33.9 %reduce-scatter.5.cloned.1.call-done = bf16[2,16,128,128]{2,1,3,0:T(8,128)(2,1)} async-done(((bf16[2,64,128,128]{2,1,3,0:T(8,128)(2,1)}), bf16[2,16,128,128]{2,1,3,0:T(8,128)(2,1)}) %reduce-scatter.5.cloned.1.call-update) | async-done | bytes 1048592 | tf_op jit(solution)/shard_map/reduce_scatter | solution.py:121
  252.2 1.5 convert_reduce_fusion.3
  253.7 1.4 copy.76
  255.1 3.6 multiply_convert_fusion.6
  258.7 0.8 copy-done.13
  259.5 1.2 convolution_bitcast_fusion
  260.7 2.0 fusion.47
  262.8 0.3 fusion.24
  263.1 1.0 copy.78
  264.1 89.8 %all-reduce.3.cloned.1.call-done = (f32[128,512]{1,0:T(8,128)}, f32[128,128]{1,0:T(8,128)}, f32[128,128]{1,0:T(8,128)}) async-done(((f32[128,512]{1,0:T(8,128)}, f32[128,128]{1,0:T(8,128)}, f32[128,128]{1,0:T(8,128)}), (f32[128,512]{1,0:T(8,128)}, f32[128,128]{1,0:T(8,128)}, f32[128,128]{1,0:T(8,128)})) %all-reduce.3.cloned.1.call-update) | async-done | bytes 393232 | tf_op jit(solution)/shard_map/psum | solution.py:141
  353.9 1.7 copy.97
  355.6 1.5 copy.98
  357.0 1.5 copy.99
  (64 shorter events, 0.7 us)
Async XLA Ops:
  7.2 1.7 copy-start
  7.2 33.2 %all-gather.3.cloned.1.call-start = ((), (), s32[]{:S(2)}) async-start(), calls=%async_computation.4 | async-start | bytes 2621440 | tf_op jit(solution)/shard_map/all_gather | solution.py:70
  10.4 1.9 copy-start.1
  12.3 7.3 %copy-start.21 = (s32[1,2]{1,0:T(1,128)S(1)}, s32[1,2]{1,0:T(1,128)}, u32[]{:S(2)}) copy-start(s32[1,2]{1,0:T(1,128)} %param.15) | copy-start | bytes 28
  12.3 18.1 %copy-start.3 = (bf16[1,2,32,128,128]{4,3,2,1,0:T(8,128)(2,1)S(1)}, bf16[1,2,32,128,128]{4,3,2,1,0:T(8,128)(2,1)}, u32[]{:S(2)}) copy-start(bf16[1,2,32,128,128]{4,3,2,1,0:T(8,128)(2,1)} %param.13) | copy-start | bytes 6291460
  13.7 19.9 %copy-start.16 = (f32[128]{0:T(128)S(1)}, f32[128]{0:T(128)}, u32[]{:S(2)}) copy-start(f32[128]{0:T(128)} %param.17) | copy-start | bytes 1540
  13.7 19.9 %copy-start.17 = (f32[128]{0:T(128)S(1)}, f32[128]{0:T(128)}, u32[]{:S(2)}) copy-start(f32[128]{0:T(128)} %param.18) | copy-start | bytes 1540
  14.6 14.9 %all-to-all-start = ((bf16[4,16,1,32,128]{4,3,1,2,0:T(8,128)(2,1)}), bf16[4,16,1,32,128]{4,3,1,2,0:T(8,128)(2,1)S(1)}, u32[]{:S(2)}, u32[]{:S(2)}) async-start(bf16[4,16,1,32,128]{4,3,1,2,0:T(8,128)(2,1)} %pad_maximum_fusion.1), calls=%async_computation | async-start | bytes 1048576 | tf_op jit(solution)/shard_map/all_to_all | solution.py:66
  18.8 70.7 %all-gather.5.cloned.1.call-start = ((), (), s32[]{:S(2)}) async-start(), calls=%async_computation.5 | async-start | bytes 2621440 | tf_op jit(solution)/shard_map/all_gather | solution.py:68
  29.5 0.8 copy-start.11
  30.3 175.5 %reduce-scatter.3.cloned.1.call-start = ((), (), s32[]{:S(2)}) async-start(), calls=%async_computation.6 | async-start | bytes 2621440 | tf_op jit(solution)/shard_map/reduce_scatter | solution.py:106
  118.2 3.4 copy-start.2
  118.2 3.4 copy-start.15
  118.2 3.5 copy-start.18
  121.0 5.2 %copy-start.14 = (bf16[128,128]{1,0:T(8,128)(2,1)S(1)}, bf16[128,128]{1,0:T(8,128)(2,1)}, u32[]{:S(2)}) copy-start(bf16[128,128]{1,0:T(8,128)(2,1)} %param.22) | copy-start | bytes 98308
  126.2 1.3 copy-start.4
  126.2 2.3 copy-start.7
  126.2 3.0 copy-start.19
  126.2 3.0 copy-start.20
  133.5 6.2 %copy-start.9 = (bf16[8192,128]{1,0:T(8,128)(2,1)}, bf16[8192,128]{1,0:T(8,128)(2,1)S(1)}, u32[]{:S(2)}) copy-start(bf16[8192,128]{1,0:T(8,128)(2,1)S(1)} %get-tuple-element.43) | copy-start | bytes 6291460
  145.2 6.2 %copy-start.6 = (bf16[64,128,128,1]{1,0,3,2:T(8,128)(2,1)S(1)}, bf16[64,128,128,1]{1,0,3,2:T(8,128)(2,1)}, u32[]{:S(2)}) copy-start(bf16[64,128,128,1]{1,0,3,2:T(8,128)(2,1)} %copy.81) | copy-start | bytes 6291460
  150.0 1.4 copy-start.5
  163.1 89.1 %reduce-scatter.5.cloned.1.call-start = ((), (), s32[]{:S(2)}) async-start(), calls=%async_computation.7 | async-start | bytes 5242880 | tf_op jit(solution)/shard_map/reduce_scatter | solution.py:121
  189.5 23.8 %copy-start.8 = (bf16[8192,128]{1,0:T(8,128)(2,1)S(1)}, bf16[8192,128]{1,0:T(8,128)(2,1)}, u32[]{:S(2)}) copy-start(bf16[8192,128]{1,0:T(8,128)(2,1)} %add_convert_fusion.1) | copy-start | bytes 6291460
  205.8 12.3 %all-to-all-start.1 = ((bf16[4,16,32,128]{3,2,1,0:T(8,128)(2,1)}), bf16[4,16,32,128]{3,2,1,0:T(8,128)(2,1)S(1)}, u32[]{:S(2)}, u32[]{:S(2)}) async-start(bf16[4,16,32,128]{3,2,1,0:T(8,128)(2,1)} %bitcast.133), calls=%async_computation.2 | async-start | bytes 1048576 | tf_op jit(solution)/shard_map/all_to_all | solution.py:109
  209.3 144.6 %all-reduce.3.cloned.1.call-start = ((), (), s32[]{:S(2)}) async-start(), calls=%async_computation.8 | async-start | bytes 786432 | tf_op jit(solution)/shard_map/psum | solution.py:141
  209.6 3.8 %copy-start.10 = (bf16[8192,128]{1,0:T(8,128)(2,1)S(1)}, bf16[8192,128]{1,0:T(8,128)(2,1)}, u32[]{:S(2)}) copy-start(bf16[8192,128]{1,0:T(8,128)(2,1)} %get-tuple-element.41) | copy-start | bytes 6291460
  258.7 0.8 copy-start.13
  258.7 2.0 copy-start.12
Sparse Core Ops, SparseCore 0:
  13.8 26.5 all-gather.2
  42.6 46.9 all-gather.4
  163.2 42.5 reduce-scatter.2
  208.3 43.8 reduce-scatter.4
  262.9 90.9 all-reduce.2
